TPU v7x, 512 devices: a whole 4x4x16 slice. The times are simulated.
512 devices in a mesh: pool: 64 (over z, x), tp: 8 (over y, core).
Axes of the slice: x: 4, y: 4, z: 16, core: 2. Of those that a mesh axis runs over, the one named last changes fastest.
Arguments:
- queries: bfloat16 [128, 8192], P('pool', 'tp'), may hold values from -12 to 12
- key_cache: bfloat16 [8, 1024, 512, 128], P('tp', 'pool'), may hold values from -12 to 12
- value_cache: bfloat16 [8, 1024, 512, 128], P('tp', 'pool'), may hold values from -8 to 8
- out_weight: bfloat16 [8192, 8192], P('tp', 'pool'), may hold values from -0.0625 to 0.0625
- lengths: int32 [128], replicated, may hold values from 1 to 16384
- block_table: int32 [128, 32], replicated, may hold values from -1 to 1023, as said below
Outputs:
- output: bfloat16 [128, 8192], P('tp', 'pool')
Inputs may be any that keep to these rules, and one draw needn't show every extreme that they name: `block_table`: entries of one row's table past its ceil(length / 512) blocks are -1, the others are distinct global slot ids, and each slot belongs to at most one row; slot s lies on index floor(s / 16) of pool.
All inputs are finite; a program needn't handle non-finite values.
Results may differ from a plain program's by a relative error of at most 0.0052.
Values may be sent and summed in bfloat16 or wider, within the bound.
A program may use at most 64 MiB of HBM per device.

v0:
```python
import math

import jax
import jax.numpy as jnp
from jax import lax
from jax.sharding import PartitionSpec as P

FLOOR = -1e30


def on_device(queries, key_cache, value_cache, out_weight, lengths, block_table):
    kv_local, slot_count, block_len, head_dim = key_cache.shape
    rows_local, features = queries.shape
    heads_local = features // head_dim
    group_size = heads_local // kv_local
    total_rows, max_blocks = block_table.shape
    scaling = 1.0 / math.sqrt(head_dim)
    everyone = lax.all_gather(queries, "pool", axis=0, tiled=True)
    lender = lax.axis_index("pool")
    slot_ids = lender * slot_count + jnp.arange(slot_count, dtype=jnp.int32)
    matches = block_table[:, :, None] == slot_ids[None, None, :]
    holder = jnp.any(matches, axis=1)
    in_use = jnp.any(holder, axis=0)
    block_of = jnp.sum(
        jnp.where(matches, jnp.arange(max_blocks, dtype=jnp.int32)[None, :, None], 0), axis=(0, 1)
    )
    length_of = jnp.sum(jnp.where(holder, lengths[:, None], 0), axis=0)
    chooser = holder.astype(jnp.bfloat16)
    picked = jnp.dot(chooser.T, everyone, preferred_element_type=jnp.float32).astype(jnp.bfloat16)
    picked = picked.reshape(slot_count, kv_local, group_size, head_dim)
    scores = (
        jnp.einsum("skgd,kstd->skgt", picked, key_cache, preferred_element_type=jnp.float32)
        * scaling
    )
    position = block_of[:, None] * block_len + jnp.arange(block_len, dtype=jnp.int32)[None, :]
    usable = (position < length_of[:, None]) & in_use[:, None]
    usable = usable[:, None, None, :]
    scores = jnp.where(usable, scores, FLOOR)
    block_max = jnp.max(scores, axis=-1)
    weights = jnp.where(usable, jnp.exp(scores - block_max[..., None]), 0.0)
    block_sum = jnp.sum(weights, axis=-1)
    block_out = jnp.einsum(
        "skgt,kstd->skgd",
        weights.astype(jnp.bfloat16),
        value_cache,
        preferred_element_type=jnp.float32,
    )
    block_max = block_max.reshape(slot_count, heads_local)
    block_sum = block_sum.reshape(slot_count, heads_local)
    block_out = block_out.reshape(slot_count, heads_local, head_dim)
    row_peak = jnp.max(jnp.where(holder[:, :, None], block_max[None], FLOOR), axis=1)
    slot_ref = jnp.max(jnp.where(holder[:, :, None], row_peak[:, None, :], FLOOR), axis=0)
    factor = jnp.exp(block_max - slot_ref)
    spread = holder.astype(jnp.float32)
    row_total = jnp.dot(spread, block_sum * factor, precision=lax.Precision.HIGHEST)
    row_part = jnp.dot(
        spread,
        (block_out * factor[..., None]).reshape(slot_count, features),
        precision=lax.Precision.HIGHEST,
    )
    got_part, got_peak, got_total = (
        lax.all_to_all(row_part[None], "pool", split_axis=1, concat_axis=0, tiled=True),
        lax.all_to_all(row_peak[None], "pool", split_axis=1, concat_axis=0, tiled=True),
        lax.all_to_all(row_total[None], "pool", split_axis=1, concat_axis=0, tiled=True),
    )
    highest = jnp.max(got_peak, axis=0)
    weight_each = jnp.exp(got_peak - highest[None])
    denominator = jnp.sum(got_total * weight_each, axis=0)
    numerator = jnp.sum(
        got_part.reshape(-1, rows_local, heads_local, head_dim) * weight_each[..., None], axis=0
    )
    attended = (
        (numerator / denominator[..., None]).reshape(rows_local, features).astype(jnp.bfloat16)
    )
    partial_value = jnp.dot(
        lax.all_gather(attended, "pool", axis=0, tiled=True),
        out_weight,
        preferred_element_type=jnp.float32,
    )
    output = lax.psum_scatter(partial_value, "tp", scatter_dimension=0, tiled=True)
    return output.astype(jnp.bfloat16)


def solution(mesh):
    return jax.shard_map(
        on_device,
        mesh=mesh,
        in_specs=(
            P("pool", "tp"),
            P("tp", "pool", None, None),
            P("tp", "pool", None, None),
            P("tp", "pool"),
            P(),
            P(),
        ),
        out_specs=P("tp", "pool"),
        check_vma=False,
    )
```

profile of v0, /device:TPU:1, one launch (start us, length us, event | category | flops | bytes accessed | tf_op | source)
XLA Modules:
  0.0 297.1 jit_solution(16555261013130707360)
XLA Ops:
  6.5 0.0 copy-start
  6.5 1.1 fusion.14
  7.6 0.9 compare_reduce_fusion
  8.6 70.2 %all-gather = bf16[64,2,1024]{2,1,0:T(2,128)(2,1)S(1)} all-gather(bf16[1,2,1024]{2,1,0:T(2,128)(2,1)} %bitcast.56), channel_id=1, replica_groups=mesh['pool'=64,'tp'=8] {'pool'}, dimensions={0}, use_global_device_ids=true | all-gather | bytes 266240 | tf_op jit(solution)/shard_map/all_gather | solution.py:18
  78.8 0.1 reshape.152
  78.9 0.8 select_reduce_fusion.2
  79.7 0.1 fusion.13
  79.8 0.1 fusion.23
  79.9 0.0 copy-done
  79.9 0.7 fusion.29
  80.6 0.1 select_reduce_fusion.1
  80.7 0.1 select_reduce_fusion
  80.9 0.2 fusion.15
  81.1 0.9 fusion.24
  81.9 9.4 %all-to-all-start.2 = ((f32[1,128,8]{2,0,1:T(1,128)}), f32[1,128,8]{2,0,1:T(1,128)S(1)}, u32[]{:S(2)}, u32[]{:S(2)}) async-start(f32[1,128,8]{2,0,1:T(1,128)} %bitcast.11), calls=%async_computation.2 | async-start | bytes 131072 | tf_op jit(solution)/shard_map/all_to_all | solution.py:64
  91.4 2.0 fusion.10
  93.4 0.7 copy.16
  94.1 11.2 %all-to-all-done.2 = f32[1,128,8]{2,0,1:T(1,128)S(1)} async-done(((f32[1,128,8]{2,0,1:T(1,128)}), f32[1,128,8]{2,0,1:T(1,128)S(1)}, u32[]{:S(2)}, u32[]{:S(2)}) %all-to-all-start.2) | async-done | bytes 4128 | tf_op jit(solution)/shard_map/all_to_all | solution.py:64
  105.3 4.6 %all-to-all-start.1 = ((f32[1,128,8]{2,0,1:T(1,128)}), f32[1,128,8]{2,0,1:T(1,128)S(1)}, u32[]{:S(2)}, u32[]{:S(2)}) async-start(f32[1,128,8]{2,0,1:T(1,128)} %copy.16), calls=%async_computation.1 | async-start | bytes 131072 | tf_op jit(solution)/shard_map/all_to_all | solution.py:63
  109.9 0.4 convolution_bitcast_fusion
  110.4 1.3 copy.15
  111.7 0.0 copy-start.1
  111.7 12.2 %all-to-all-done.1 = f32[1,128,8]{2,0,1:T(1,128)S(1)} async-done(((f32[1,128,8]{2,0,1:T(1,128)}), f32[1,128,8]{2,0,1:T(1,128)S(1)}, u32[]{:S(2)}, u32[]{:S(2)}) %all-to-all-start.1) | async-done | bytes 4128 | tf_op jit(solution)/shard_map/all_to_all | solution.py:63
  123.9 4.6 %all-to-all-start = ((f32[1,128,1024]{2,0,1:T(1,128)}), f32[1,128,1024]{2,0,1:T(1,128)S(1)}, u32[]{:S(2)}, u32[]{:S(2)}) async-start(f32[1,128,1024]{2,0,1:T(1,128)} %copy.15), calls=%async_computation | async-start | bytes 1048576 | tf_op jit(solution)/shard_map/all_to_all | solution.py:62
  128.5 0.0 reduce-scatter.2.cloned.1.call-start
  128.6 0.1 reduce_max.39
  128.6 0.1 multiply_reduce_fusion.1
  128.7 0.1 broadcast_bitcast_fusion
  128.8 23.0 %all-to-all-done = f32[1,128,1024]{2,0,1:T(1,128)S(1)} async-done(((f32[1,128,1024]{2,0,1:T(1,128)}), f32[1,128,1024]{2,0,1:T(1,128)S(1)}, u32[]{:S(2)}, u32[]{:S(2)}) %all-to-all-start) | async-done | bytes 524320 | tf_op jit(solution)/shard_map/all_to_all | solution.py:62
  151.8 0.2 mul.66
  152.0 0.6 multiply_reduce_fusion
  152.6 67.0 %all-gather.1 = bf16[64,2,1024]{2,1,0:T(2,128)(2,1)S(1)} all-gather(bf16[1,2,1024]{2,1,0:T(2,128)(2,1)S(1)} %fusion.27), channel_id=1, replica_groups=mesh['pool'=64,'tp'=8] {'pool'}, dimensions={0}, use_global_device_ids=true | all-gather | bytes 266240 | tf_op jit(solution)/shard_map/all_gather | solution.py:76
  219.5 0.1 reshape.154
  219.6 0.0 copy-done.1
  219.7 0.8 fusion.30
  220.5 0.0 reduce-scatter.2.cloned.1.call-update
  220.5 68.4 %reduce-scatter.2.cloned.1.call-done = f32[16,128]{1,0:T(8,128)} async-done(((f32[128,128]{1,0:T(8,128)}), f32[16,128]{1,0:T(8,128)}) %reduce-scatter.2.cloned.1.call-update) | async-done | bytes 8208 | tf_op jit(solution)/shard_map/reduce_scatter | solution.py:80
  289.0 1.3 convert_element_type.18
  (5 shorter events, 0.0 us)
Async XLA Ops:
  6.5 73.4 %copy-start = (bf16[1,16,512,128]{3,2,1,0:T(8,128)(2,1)S(1)}, bf16[1,16,512,128]{3,2,1,0:T(8,128)(2,1)}, u32[]{:S(2)}) copy-start(bf16[1,16,512,128]{3,2,1,0:T(8,128)(2,1)} %param.7) | copy-start | bytes 6291460
  81.9 23.4 %all-to-all-start.2 = ((f32[1,128,8]{2,0,1:T(1,128)}), f32[1,128,8]{2,0,1:T(1,128)S(1)}, u32[]{:S(2)}, u32[]{:S(2)}) async-start(f32[1,128,8]{2,0,1:T(1,128)} %bitcast.11), calls=%async_computation.2 | async-start | bytes 131072 | tf_op jit(solution)/shard_map/all_to_all | solution.py:64
  105.3 18.6 %all-to-all-start.1 = ((f32[1,128,8]{2,0,1:T(1,128)}), f32[1,128,8]{2,0,1:T(1,128)S(1)}, u32[]{:S(2)}, u32[]{:S(2)}) async-start(f32[1,128,8]{2,0,1:T(1,128)} %copy.16), calls=%async_computation.1 | async-start | bytes 131072 | tf_op jit(solution)/shard_map/all_to_all | solution.py:63
  111.7 108.0 %copy-start.1 = (bf16[1024,128]{1,0:T(8,128)(2,1)S(1)}, bf16[1024,128]{1,0:T(8,128)(2,1)}, u32[]{:S(2)}) copy-start(bf16[1024,128]{1,0:T(8,128)(2,1)} %param.9) | copy-start | bytes 786436
  123.9 27.9 %all-to-all-start = ((f32[1,128,1024]{2,0,1:T(1,128)}), f32[1,128,1024]{2,0,1:T(1,128)S(1)}, u32[]{:S(2)}, u32[]{:S(2)}) async-start(f32[1,128,1024]{2,0,1:T(1,128)} %copy.15), calls=%async_computation | async-start | bytes 1048576 | tf_op jit(solution)/shard_map/all_to_all | solution.py:62
  128.5 160.5 %reduce-scatter.2.cloned.1.call-start = ((), (), s32[]{:S(2)}) async-start(), calls=%async_computation.4 | async-start | bytes 73728 | tf_op jit(solution)/shard_map/reduce_scatter | solution.py:80
Sparse Core Ops, SparseCore 0:
  220.6 68.2 reduce-scatter.1
where the time goes:
time: 298 us; the launch traced here: 297 us
  blocking collectives  137 us (46%)
  waiting for transfers between devices  115 us (39%)
  starting transfers between devices  18.7 us (6%)
  between operations  13.5 us (5%)
  other arithmetic  5.32 us (2%)
  matrix products  5.02 us (2%)
    all_gather x1, blocking collectives, on_device(): everyone = lax.all_gather(queries, 'pool', axis=0, tiled=True)  70.2 us
    reduce_scatter x1, waiting for transfers between devices, on_device(): lax.psum_scatter(partial_value, 'tp', scatter_dimension=0, tiled=True)  68.4 us
    all_gather x1, blocking collectives, on_device(): lax.all_gather(attended, 'pool', axis=0, tiled=True)  67 us
    all_to_all x1, waiting for transfers between devices, on_device(): lax.all_to_all(row_part[None], 'pool', split_axis=1, concat_axis=0, tiled...  23 us
    all_to_all x1, waiting for transfers between devices, on_device(): lax.all_to_all(row_peak[None], 'pool', split_axis=1, concat_axis=0, tiled...  12.2 us
    all_to_all x1, waiting for transfers between devices, on_device(): lax.all_to_all(row_total[None], 'pool', split_axis=1, concat_axis=0, tile...  11.2 us
    all_to_all x1, starting transfers between devices, on_device(): lax.all_to_all(row_total[None], 'pool', split_axis=1, concat_axis=0, tile...  9.43 us
  transfers between devices with their start and end apart: 4, of which 4 were waited for; matrix products, arithmetic and copies ran while one was open for 2% of the time, Pallas kernels for 0%

commit v1 on v0

v1 whole, which is shorter than its diff:
```python
import functools
import math

import jax
import jax.numpy as jnp
from jax import lax
from jax.experimental import pallas as pl
from jax.experimental.pallas import tpu as pltpu
from jax.sharding import PartitionSpec as P

MESH = pl.DeviceIdType.MESH
FLOOR = -1e30
F32 = jnp.float32
BF16 = jnp.bfloat16

NZ, NX, NT = 16, 4, 8
ROWS, SLOTS, BLK, HD, GROUP, MAXB = 128, 16, 512, 128, 8, 32
PAIR = GROUP // NX
BAND = ROWS // NT
NEAR = 4
ZORDER = [(k - NEAR) % NZ for k in range(NZ)]
NEAR_N = 2 * NEAR + 1
FAR_FIRST = [8, 7, 9, 6, 10, 5, 11, 4, 12, 3, 13, 2, 14, 1, 15]


def dot(a, b, dims=((1,), (0,))):
    return lax.dot_general(a, b, (dims, ((), ())), preferred_element_type=F32)


def kernel(
    q_hbm,
    k_hbm,
    v_hbm,
    w_hbm,
    len_hbm,
    tab_hbm,
    out_ref,
    tab,
    lens,
    keys,
    vals,
    qall,
    sel,
    lims,
    hold,
    prob,
    o_f,
    stat_f,
    o_send,
    st_x,
    o_x,
    zst_send,
    zst,
    scale_t,
    zw,
    part,
    rs,
    att,
    wx,
    pl_send,
    pl_recv,
    loc_sem,
    sq,
    rq,
    sqx,
    rqx,
    sw,
    rw,
    sst,
    rst,
    so,
    ro,
    szs,
    rzs,
    srs,
    rrs,
    sag,
    rag,
    spl,
    rpl,
):
    pool = lax.axis_index("pool")
    t = lax.axis_index("tp")
    z = pool // NX
    x = pool % NX

    def at(dz, dx, dt):
        return {
            "pool": ((z + dz) % NZ) * NX + (x + dx) % NX,
            "tp": (t + dt) % NT,
        }

    def remote(src, dst, send, recv, to):
        copy = pltpu.make_async_remote_copy(
            src_ref=src,
            dst_ref=dst,
            send_sem=send,
            recv_sem=recv,
            device_id=to,
            device_id_type=MESH,
        )
        copy.start()
        return copy

    sends = []

    own = NEAR
    c_tab = pltpu.make_async_copy(tab_hbm, tab, loc_sem.at[0])
    c_len = pltpu.make_async_copy(len_hbm, lens, loc_sem.at[1])
    c_q = pltpu.make_async_copy(q_hbm, qall.at[0, own], loc_sem.at[2])
    c_k = pltpu.make_async_copy(k_hbm.at[0], keys, loc_sem.at[3])
    c_v = pltpu.make_async_copy(v_hbm.at[0], vals, loc_sem.at[4])
    c_w = pltpu.make_async_copy(
        w_hbm.at[pl.ds(pl.multiple_of(x * PAIR * HD, PAIR * HD), PAIR * HD)],
        wx.at[0],
        loc_sem.at[5],
    )
    plane = [(dx, dt) for dx in range(NX) for dt in range(NT) if (dx, dt) != (0, 0)]
    barrier = pltpu.get_barrier_semaphore()
    for dz in FAR_FIRST:
        pl.semaphore_signal(barrier, inc=1, device_id=at(dz, 0, 0), device_id_type=MESH)
    for dx, dt in plane:
        pl.semaphore_signal(barrier, inc=1, device_id=at(0, dx, dt), device_id_type=MESH)
    c_q.start()
    c_tab.start()
    c_len.start()
    c_k.start()
    c_v.start()
    c_w.start()

    c_tab.wait()
    c_len.wait()
    tab_t = tab[...].astype(F32)
    len_row = lens[...].astype(F32)
    sub = lax.broadcasted_iota(jnp.int32, (ROWS, ROWS), 0)
    lane = lax.broadcasted_iota(jnp.int32, (ROWS, ROWS), 1)
    sid = (pool * SLOTS + sub // GROUP).astype(F32)
    left = jnp.zeros((ROWS, ROWS), F32)
    sub4 = lax.broadcasted_iota(jnp.int32, (NX * SLOTS, ROWS), 0)
    sid4 = ((z * NX + (x + sub4 // SLOTS) % NX) * SLOTS + sub4 % SLOTS).astype(F32)
    held = jnp.zeros((NX * SLOTS, ROWS), F32)
    for b in range(MAXB):
        entry = tab_t[b : b + 1, :]
        left = jnp.where(entry == sid, len_row - float(BLK * b), left)
        held = jnp.where(entry == sid4, 1.0, held)
    hold[...] = held
    lims[...] = jnp.broadcast_to(jnp.sum(left, axis=1, keepdims=True), (ROWS, ROWS))
    row_of = jnp.sum(
        jnp.where(left > 0.0, (lane + 1).astype(F32), 0.0), axis=1, keepdims=True
    )
    key_col = (row_of - 1.0) * float(GROUP) + (sub[:, 0:1] % GROUP).astype(F32)
    j = lax.broadcasted_iota(jnp.int32, (1, ROWS * GROUP), 1)
    piece = j // 16
    dx_j = piece // NZ
    dz_j = piece % NZ - NEAR + NZ
    p_j = ((z + dz_j) % NZ) * NX + (x + dx_j) % NX
    key_row = ((2 * p_j + j % 2) * GROUP + (j % 16) // 2).astype(F32)
    for c in range(8):
        cut = slice(c * 128, (c + 1) * 128)
        sel[:, cut] = jnp.where(key_col == key_row[:, cut], 1.0, 0.0).astype(BF16)
    c_q.wait()
    pl.semaphore_wait(barrier, len(FAR_FIRST) + len(plane))

    place = {dz: k for k, dz in enumerate(ZORDER)}
    got = {}
    for dz in FAR_FIRST:
        k = place[(NZ - dz) % NZ]
        got[k] = remote(
            qall.at[0, own], qall.at[0, k], sq.at[dz], rq.at[k], at(dz, 0, 0)
        )
        sends.append(got[k])
    xgot = []
    for lo, hi, s in ((0, NEAR_N, 0), (NEAR_N, NZ, 1)):
        for k in range(lo, hi):
            if k != own:
                got[k].wait_recv()
        for dx in (2, 1, 3):
            e = (NX - dx) % NX
            copy = remote(
                qall.at[0, pl.ds(lo, hi - lo)],
                qall.at[e, pl.ds(lo, hi - lo)],
                sqx.at[dx, s],
                rqx.at[e, s],
                at(0, dx, 0),
            )
            xgot.append(copy)
            sends.append(copy)
    wgot = []
    for dx in (2, 1, 3):
        e = (NX - dx) % NX
        rows = pl.ds(pl.multiple_of(((x + dx) % NX) * PAIR * HD, PAIR * HD), PAIR * HD)
        copy = remote(w_hbm.at[rows], wx.at[e], sw.at[dx], rw.at[e], at(0, dx, 0))
        wgot.append(copy)
        sends.append(copy)
    c_k.wait()
    for copy in xgot:
        copy.wait_recv()

    picked = dot(sel[...], qall[...].reshape(ROWS * GROUP, HD))
    scaling = 1.0 / math.sqrt(HD)
    place_in = lax.broadcasted_iota(jnp.int32, (GROUP, BLK), 1).astype(F32)
    lane8 = lax.broadcasted_iota(jnp.int32, (GROUP, HD), 1)
    for s in range(SLOTS):
        mine = slice(GROUP * s, GROUP * (s + 1))
        scores = dot(picked[mine].astype(BF16), keys[s], ((1,), (1,))) * scaling
        usable = place_in < lims[mine, 0:1]
        scores = jnp.where(usable, scores, FLOOR)
        peak = jnp.max(scores, axis=1, keepdims=True)
        weights = jnp.where(usable, jnp.exp(scores - peak), 0.0)
        total = jnp.sum(weights, axis=1, keepdims=True)
        prob[s] = weights.astype(BF16)
        stat_f[pl.ds(s, GROUP, stride=SLOTS), :] = jnp.where(lane8 == 0, peak, total)
    mine_x = pl.ds(pl.multiple_of(x * PAIR * SLOTS, PAIR * SLOTS), PAIR * SLOTS)
    stgot = []
    for dx in (2, 1, 3):
        e = (NX - dx) % NX
        rows = pl.ds(pl.multiple_of(((x + dx) % NX) * PAIR * SLOTS, PAIR * SLOTS), PAIR * SLOTS)
        copy = remote(stat_f.at[rows], st_x.at[e], sst.at[dx], rst.at[e], at(0, dx, 0))
        stgot.append(copy)
        sends.append(copy)
    st_x[0] = stat_f[mine_x, :]
    c_v.wait()
    for s in range(SLOTS):
        o_f[pl.ds(s, GROUP, stride=SLOTS), :] = dot(prob[s], vals[s])
    o_send[...] = o_f[...].astype(BF16)
    ogot = []
    for dx in (2, 1, 3):
        e = (NX - dx) % NX
        rows = pl.ds(pl.multiple_of(((x + dx) % NX) * PAIR * SLOTS, PAIR * SLOTS), PAIR * SLOTS)
        copy = remote(o_send.at[rows], o_x.at[e], so.at[dx], ro.at[e], at(0, dx, 0))
        ogot.append(copy)
        sends.append(copy)
    o_x[0] = o_send[mine_x, :]

    for copy in stgot:
        copy.wait_recv()
    ws = []
    is_held = hold[...] > 0.0
    for hh in range(PAIR):
        cut = slice(hh * SLOTS, (hh + 1) * SLOTS)
        peak = jnp.concatenate([st_x[e, cut, 0:1] for e in range(NX)], axis=0)
        total = jnp.concatenate([st_x[e, cut, 1:2] for e in range(NX)], axis=0)
        top = jnp.max(jnp.where(is_held, peak, FLOOR), axis=0, keepdims=True)
        w = jnp.where(is_held, jnp.exp(peak - top), 0.0)
        ws.append(w.astype(BF16))
        zst_send[hh : hh + 1, :] = top
        zst_send[PAIR + hh : PAIR + hh + 1, :] = jnp.sum(w * total, axis=0, keepdims=True)
    zgot = []
    for dz in FAR_FIRST:
        e = NZ - dz
        copy = remote(zst_send, zst.at[e], szs.at[dz], rzs.at[e], at(dz, 0, 0))
        zgot.append(copy)
        sends.append(copy)
    zst[0] = zst_send[...]

    for copy in ogot:
        copy.wait_recv()
    for hh in range(PAIR):
        data = jnp.concatenate(
            [o_x[e, hh * SLOTS : (hh + 1) * SLOTS, :] for e in range(NX)], axis=0
        )
        part[:, hh * HD : (hh + 1) * HD] = dot(ws[hh], data, ((0,), (0,))).astype(BF16)
    rgot = []
    for dz in FAR_FIRST:
        e = NZ - dz
        band = ((z + dz) % NZ) % NT
        rows = pl.ds(pl.multiple_of(band * BAND, BAND), BAND)
        copy = remote(part.at[rows], rs.at[e], srs.at[dz], rrs.at[e], at(dz, 0, 0))
        rgot.append(copy)
        sends.append(copy)
    my_band = pl.ds(pl.multiple_of((z % NT) * BAND, BAND), BAND)
    rs[0] = part[my_band, :]

    for copy in zgot:
        copy.wait_recv()
    scales = []
    for hh in range(PAIR):
        top = jnp.concatenate([zst[e, hh : hh + 1, :] for e in range(NZ)], axis=0)
        total = jnp.concatenate(
            [zst[e, PAIR + hh : PAIR + hh + 1, :] for e in range(NZ)], axis=0
        )
        highest = jnp.max(top, axis=0, keepdims=True)
        w = jnp.exp(top - highest)
        scales.append(w / jnp.sum(w * total, axis=0, keepdims=True))
    pad = jnp.zeros((ROWS - PAIR * NZ, ROWS), F32)
    scale_t[...] = jnp.transpose(jnp.concatenate(scales + [pad], axis=0))
    mine = scale_t[my_band, :]
    for e in range(NZ):
        for hh in range(PAIR):
            zw[e, :, hh * HD : (hh + 1) * HD] = jnp.broadcast_to(
                mine[:, hh * NZ + e : hh * NZ + e + 1], (BAND, HD)
            )
    for copy in rgot:
        copy.wait_recv()
    acc = jnp.zeros((BAND, PAIR * HD), F32)
    for e in range(NZ):
        acc = acc + rs[e].astype(F32) * zw[e]
    att[my_band, :] = acc.astype(BF16)

    agot = []
    for dz in (4, 3, 13, 2, 14, 1, 15):
        copy = remote(att.at[my_band], att.at[my_band], sag.at[dz], rag.at[dz], at(dz, 0, 0))
        agot.append((dz, copy))
        sends.append(copy)
    c_w.wait()
    for copy in wgot:
        copy.wait_recv()
    for dz, copy in agot:
        band = ((z - dz + NZ) % NZ) % NT
        rows = pl.ds(pl.multiple_of(band * BAND, BAND), BAND)
        pltpu.make_async_copy(att.at[rows], att.at[rows], rag.at[dz]).wait()

    pgot = []
    for dx in (2, 1, 3, 0):
        pl_send[dx] = dot(att[...], wx[dx]).astype(BF16)
        for dt in (4, 5, 3, 2, 6, 1, 7, 0):
            if (dx, dt) == (0, 0):
                continue
            rows = pl.ds(pl.multiple_of(((t + dt) % NT) * BAND, BAND), BAND)
            e = ((NX - dx) % NX) * NT + (NT - dt) % NT
            copy = remote(
                pl_send.at[dx, rows],
                pl_recv.at[e],
                spl.at[dx * NT + dt],
                rpl.at[e],
                at(0, dx, dt),
            )
            pgot.append(copy)
            sends.append(copy)
    rows = pl.ds(pl.multiple_of(t * BAND, BAND), BAND)
    acc = pl_send[0, rows, :].astype(F32)
    for copy in pgot:
        copy.wait_recv()
    for e in range(1, NX * NT):
        acc = acc + pl_recv[e].astype(F32)
    out_ref[...] = acc.astype(BF16)
    for copy in sends:
        copy.wait_send()


def on_device(queries, key_cache, value_cache, out_weight, lengths, block_table):
    q = queries.reshape(2, GROUP, HD).transpose(1, 0, 2).reshape(2 * GROUP, HD)
    hbm = pl.BlockSpec(memory_space=pltpu.HBM)
    dma = pltpu.SemaphoreType.DMA
    vmem = pltpu.VMEM
    return pl.pallas_call(
        kernel,
        out_shape=jax.ShapeDtypeStruct((BAND, HD), BF16),
        in_specs=[hbm] * 6,
        out_specs=pl.BlockSpec(memory_space=pltpu.VMEM),
        scratch_shapes=[
            vmem((MAXB, ROWS), jnp.int32),
            vmem((1, ROWS), jnp.int32),
            vmem((SLOTS, BLK, HD), BF16),
            vmem((SLOTS, BLK, HD), BF16),
            vmem((NX, NZ, 2 * GROUP, HD), BF16),
            vmem((ROWS, ROWS * GROUP), BF16),
            vmem((ROWS, ROWS), F32),
            vmem((NX * SLOTS, ROWS), F32),
            vmem((SLOTS, GROUP, BLK), BF16),
            vmem((ROWS, HD), F32),
            vmem((ROWS, HD), F32),
            vmem((ROWS, HD), BF16),
            vmem((NX, PAIR * SLOTS, HD), F32),
            vmem((NX, PAIR * SLOTS, HD), BF16),
            vmem((8, ROWS), F32),
            vmem((NZ, 8, ROWS), F32),
            vmem((ROWS, ROWS), F32),
            vmem((NZ, BAND, PAIR * HD), F32),
            vmem((ROWS, PAIR * HD), BF16),
            vmem((NZ, BAND, PAIR * HD), BF16),
            vmem((ROWS, PAIR * HD), BF16),
            vmem((NX, PAIR * HD, HD), BF16),
            vmem((NX, ROWS, HD), BF16),
            vmem((NX * NT, BAND, HD), BF16),
            dma((6,)),
            dma((NZ,)),
            dma((NZ,)),
            dma((NX, 2)),
            dma((NX, 2)),
            dma((NX,)),
            dma((NX,)),
            dma((NX,)),
            dma((NX,)),
            dma((NX,)),
            dma((NX,)),
            dma((NZ,)),
            dma((NZ,)),
            dma((NZ,)),
            dma((NZ,)),
            dma((NZ,)),
            dma((NZ,)),
            dma((NX * NT,)),
            dma((NX * NT,)),
        ],
        compiler_params=pltpu.CompilerParams(
            collective_id=0, has_side_effects=True, vmem_limit_bytes=56 * 1024 * 1024
        ),
        cost_estimate=pl.CostEstimate(
            flops=400_000_000, bytes_accessed=5_000_000, transcendentals=70_000
        ),
        name="lent_attention",
    )(q, key_cache, value_cache, out_weight, lengths.reshape(1, ROWS), block_table.T)


def solution(mesh):
    return jax.shard_map(
        on_device,
        mesh=mesh,
        in_specs=(
            P("pool", "tp"),
            P("tp", "pool", None, None),
            P("tp", "pool", None, None),
            P("tp", "pool"),
            P(),
            P(),
        ),
        out_specs=P("tp", "pool"),
        check_vma=False,
    )
```

time: 298 us -> 57 us (0.19)
  blocking collectives: 137 us -> 0 us
  waiting for transfers between devices: 115 us -> 0 us
  Pallas kernels: 0 us -> 55.6 us
  starting transfers between devices: 18.7 us -> 0 us
  between operations: 13.5 us -> 0.01 us
  other arithmetic: 5.32 us -> 0 us
  matrix products: 5.02 us -> 0 us
    all_gather x2 -> x0, blocking collectives: 137 us -> none  [the longest x1 70.2 us: on_device(): everyone = lax.all_gather(queries, 'pool', axis=0, tiled=True)]
    reduce_scatter x1 -> x0, waiting for transfers between devices: 68.4 us -> none  [on_device(): lax.psum_scatter(partial_value, 'tp', scatter_dimension=0, tiled=True)]
    pallas_call x0 -> x1, Pallas kernels: none -> 55.6 us  [on_device(): pl.pallas_call(kernel, out_shape=jax.ShapeDtypeStruct((BAND, HD), BF16),...]
    all_to_all x3 -> x0, waiting for transfers between devices: 46.3 us -> none  [the longest x1 23 us: on_device(): lax.all_to_all(row_part[None], 'pool', split_axis=1, concat_axis=0, tiled...]
    all_to_all x3 -> x0, starting transfers between devices: 18.7 us -> none  [the longest x1 9.43 us: on_device(): lax.all_to_all(row_total[None], 'pool', split_axis=1, concat_axis=0, tile...]
    dot_general x6 -> x0, matrix products: 5.02 us -> none  [the longest x1 2.02 us: on_device(): jnp.einsum('skgt,kstd->skgd', weights.astype(jnp.bfloat16), value_cache,...]
  transfers between devices with their start and end apart: 4 -> 0, of which waited for: 4 -> 0; matrix products, arithmetic and copies ran while one was open for 2% -> 0% of each run, Pallas kernels for 0% -> 0%
where the time goes in v1:
time: 57 us; the launch traced here: 56.9 us
  Pallas kernels  55.6 us (98%)
  local copies, waits for them, and re-layouts  1.28 us (2%)
    pallas_call x1, Pallas kernels, on_device(): pl.pallas_call(kernel, out_shape=jax.ShapeDtypeStruct((BAND, HD), BF16),...  55.6 us
    unnamed x1, local copies, waits for them, and re-layouts  1.28 us

profile of v1, /device:TPU:1, one launch (start us, length us, event | category | flops | bytes accessed | tf_op | source)
XLA Modules:
  0.0 56.9 jit_solution(2659036657650203251)
XLA Ops:
  0.0 55.6 %lent_attention.1 = bf16[16,128]{1,0:T(8,128)(2,1)} custom-call(bf16[16,128]{1,0:T(8,128)(2,1)} %bitcast.8, bf16[1,16,512,128]{3,2,1,0:T(8,128)(2,1)} %k_hbm.1, bf16[1,16,512,128]{3,2,1,0:T(8,128)(2,1)} %v_hbm.1, bf16[1024,128]{1,0:T(8,128)(2,1)} %w_hbm.1, s32[1,128]{1,0:T(1,128)} %bitcast.9, s32[32,128]{1,0:T(8,128)} %bitcast.7), custom_call_target="tpu_custom_call" | custom-call | flops 400000000 | bytes 5000000 | tf_op jit(solution)/shard_map/lent_attention/pallas_call | solution.py:346
  55.6 1.3 %copy.9 = bf16[16,128]{1,0:T(8,128)(2,1)} copy(bf16[16,128]{1,0:T(8,128)(2,1)} %lent_attention.1) | data formatting | bytes 8192

commit v2 on v1

v2 whole, which is shorter than its diff:
```python
import functools
import math

import jax
import jax.numpy as jnp
from jax import lax
from jax.experimental import pallas as pl
from jax.experimental.pallas import tpu as pltpu
from jax.sharding import PartitionSpec as P

MESH = pl.DeviceIdType.MESH
FLOOR = -1e30
F32 = jnp.float32
BF16 = jnp.bfloat16

NZ, NX, NT = 16, 4, 8
ROWS, SLOTS, BLK, HD, GROUP, MAXB = 128, 16, 512, 128, 8, 32
PAIR = GROUP // NX
BAND = ROWS // NT
ZORDER = [0, 1, 2, 3, 4, 15, 14, 13, 12, 5, 6, 11, 10, 7, 8, 9]
LEGS = ((0, 9), (9, 13), (13, 16))
FAR_FIRST = (8, 7, 9, 6, 10, 5, 11, 4, 12, 3, 13, 2, 14, 1, 15)
ENDS = sorted(
    [(dz, dx) for dz in range(-3, 5) for dx in range(NX)],
    key=lambda d: -(abs(d[0]) + min(d[1], NX - d[1])),
)


def dot(a, b, dims=((1,), (0,))):
    return lax.dot_general(a, b, (dims, ((), ())), preferred_element_type=F32)


def kernel(
    q_hbm,
    k_hbm,
    v_hbm,
    w_hbm,
    len_hbm,
    tab_hbm,
    out_ref,
    tab,
    lens,
    keys,
    keys_t,
    vals,
    qall,
    sel,
    lims,
    hold,
    score,
    prob,
    o_f,
    stat_f,
    o_send,
    st_x,
    o_x,
    zst_send,
    zst,
    scale_t,
    zw,
    part,
    rs,
    band,
    fin,
    wall,
    loc_sem,
    sq,
    rq,
    sqx,
    rqx,
    sw,
    rw,
    sst,
    rst,
    so,
    ro,
    szs,
    rzs,
    srs,
    rrs,
    sfin,
    rfin,
    seen,
):
    pool = lax.axis_index("pool")
    t = lax.axis_index("tp")
    z = pool // NX
    x = pool % NX
    mine = (z + 3 * t) % NT

    def at(dz, dx):
        return {"pool": ((z + dz) % NZ) * NX + (x + dx) % NX, "tp": t}

    def remote(src, dst, send, recv, to):
        copy = pltpu.make_async_remote_copy(
            src_ref=src,
            dst_ref=dst,
            send_sem=send,
            recv_sem=recv,
            device_id=to,
            device_id_type=MESH,
        )
        copy.start()
        return copy

    def rows_of(index, size):
        return pl.ds(pl.multiple_of(index * size, size), size)

    def arrived(ref, sem):
        pltpu.make_async_copy(ref, ref, sem).wait()

    barrier = pltpu.get_barrier_semaphore()
    for dz in FAR_FIRST:
        pl.semaphore_signal(barrier, inc=1, device_id=at(dz, 0), device_id_type=MESH)
    c_q = pltpu.make_async_copy(q_hbm, qall.at[0, 0], loc_sem.at[2])
    c_q.start()
    for dt in (4, 3, 5, 2, 6, 1, 7):
        pl.semaphore_signal(
            barrier, inc=1, device_id={"pool": pool, "tp": (t + dt) % NT}, device_id_type=MESH
        )
    for dx in (2, 1, 3):
        pl.semaphore_signal(barrier, inc=1, device_id=at(0, dx), device_id_type=MESH)
    c_tab = pltpu.make_async_copy(tab_hbm, tab, loc_sem.at[0])
    c_len = pltpu.make_async_copy(len_hbm, lens, loc_sem.at[1])
    c_k = pltpu.make_async_copy(k_hbm.at[0], keys, loc_sem.at[3])
    c_v = pltpu.make_async_copy(v_hbm.at[0], vals, loc_sem.at[4])
    c_w = pltpu.make_async_copy(w_hbm, wall.at[t], loc_sem.at[5])
    c_tab.start()
    c_len.start()
    c_k.start()
    c_v.start()
    c_w.start()
    c_q.wait()
    pl.semaphore_wait(barrier, NZ - 1 + NX - 1 + NT - 1)

    place = {dz: k for k, dz in enumerate(ZORDER)}
    leg_of = [n for n, (lo, hi) in enumerate(LEGS) for k in range(lo, hi)]
    for dz in FAR_FIRST:
        k = place[NZ - dz]
        remote(qall.at[0, 0], qall.at[0, k], sq, rq.at[leg_of[k]], at(dz, 0))
    sibling = {"pool": pool, "tp": t + 1 - 2 * (t % 2)}
    for dt in (2, 6, 4):
        remote(w_hbm, wall.at[t], sw.at[0], rw.at[0], {"pool": pool, "tp": (t + dt) % NT})
    remote(w_hbm, wall.at[t], sw.at[1], rw.at[1], sibling)

    c_tab.wait()
    c_len.wait()
    tab_t = tab[...].astype(F32)
    len_row = lens[...].astype(F32)
    sub = lax.broadcasted_iota(jnp.int32, (ROWS, ROWS), 0)
    lane = lax.broadcasted_iota(jnp.int32, (ROWS, ROWS), 1)
    sid = (pool * SLOTS + sub // GROUP).astype(F32)
    left = jnp.zeros((ROWS, ROWS), F32)
    sub4 = lax.broadcasted_iota(jnp.int32, (NX * SLOTS, ROWS), 0)
    sid4 = ((z * NX + (x + sub4 // SLOTS) % NX) * SLOTS + sub4 % SLOTS).astype(F32)
    held = jnp.zeros((NX * SLOTS, ROWS), F32)
    for b in range(MAXB):
        entry = tab_t[b : b + 1, :]
        left = jnp.where(entry == sid, len_row - float(BLK * b), left)
        held = jnp.where(entry == sid4, 1.0, held)
    hold[...] = held
    lims[...] = jnp.broadcast_to(jnp.sum(left, axis=1, keepdims=True), (ROWS, ROWS))
    row_of = jnp.sum(
        jnp.where(left > 0.0, (lane + 1).astype(F32), 0.0), axis=1, keepdims=True
    )
    key_col = (row_of - 1.0) * float(GROUP) + (sub[:, 0:1] % GROUP).astype(F32)
    j = lax.broadcasted_iota(jnp.int32, (1, ROWS * GROUP), 1)
    piece = j // (2 * GROUP)
    k_j = piece % NZ
    dz_j = jnp.zeros_like(j)
    for k, dz in enumerate(ZORDER):
        dz_j = jnp.where(k_j == k, dz, dz_j)
    p_j = ((z + dz_j) % NZ) * NX + (x + piece // NZ) % NX
    key_row = ((2 * p_j + j % 2) * GROUP + (j % (2 * GROUP)) // 2).astype(F32)
    for c in range(8):
        cut = slice(c * 128, (c + 1) * 128)
        sel[:, cut] = jnp.where(key_col == key_row[:, cut], 1.0, 0.0).astype(BF16)

    for lo, hi in LEGS:
        new = max(lo, 1)
        arrived(qall.at[0, pl.ds(new, hi - new)], rq.at[LEGS.index((lo, hi))])
        for dx in (2, 1, 3):
            cut = pl.ds(lo, hi - lo)
            remote(qall.at[0, cut], qall.at[(NX - dx) % NX, cut], sqx, rqx, at(0, dx))
    c_k.wait()
    for s in range(SLOTS):
        keys_t[s] = keys[s].T
    arrived(qall.at[pl.ds(1, NX - 1)], rqx)
    teller = 3 * (t - z + NZ) % NT

    @pl.when(teller != t)
    def _():
        pl.semaphore_signal(
            seen, inc=1, device_id={"pool": pool, "tp": teller}, device_id_type=MESH
        )

    picked = dot(sel[...], qall[...].reshape(ROWS * GROUP, HD))
    scaling = 1.0 / math.sqrt(HD)
    for s in range(SLOTS):
        cut = slice(GROUP * s, GROUP * (s + 1))
        score[cut] = dot(picked[cut].astype(BF16), keys_t[s])
    each = 4
    place_in = lax.broadcasted_iota(jnp.int32, (each * GROUP, BLK), 1).astype(F32)
    first = lax.broadcasted_iota(jnp.int32, (GROUP, HD), 1) == 0
    for c in range(SLOTS // each):
        cut = slice(each * GROUP * c, each * GROUP * (c + 1))
        usable = place_in < lims[cut, 0:1]
        scores = jnp.where(usable, score[cut] * scaling, FLOOR)
        peak = jnp.max(scores, axis=1, keepdims=True)
        weights = jnp.where(usable, jnp.exp(scores - peak), 0.0)
        total = jnp.sum(weights, axis=1, keepdims=True)
        for i in range(each):
            s = each * c + i
            sl = slice(GROUP * i, GROUP * (i + 1))
            prob[s] = weights[sl].astype(BF16)
            stat_f[pl.ds(s, GROUP, stride=SLOTS), :] = jnp.where(first, peak[sl], total[sl])
    mine_x = rows_of(x, PAIR * SLOTS)
    for dx in (2, 1, 3):
        rows = rows_of((x + dx) % NX, PAIR * SLOTS)
        remote(stat_f.at[rows], st_x.at[(NX - dx) % NX], sst, rst, at(0, dx))
    st_x[0] = stat_f[mine_x, :]
    c_v.wait()
    for s in range(SLOTS):
        o_f[pl.ds(s, GROUP, stride=SLOTS), :] = dot(prob[s], vals[s])
    o_send[...] = o_f[...].astype(BF16)
    for dx in (2, 1, 3):
        rows = rows_of((x + dx) % NX, PAIR * SLOTS)
        remote(o_send.at[rows], o_x.at[(NX - dx) % NX], so, ro, at(0, dx))
    o_x[0] = o_send[mine_x, :]

    arrived(st_x.at[pl.ds(1, NX - 1)], rst)
    ws = []
    is_held = hold[...] > 0.0
    for hh in range(PAIR):
        cut = slice(hh * SLOTS, (hh + 1) * SLOTS)
        peak = jnp.concatenate([st_x[e, cut, 0:1] for e in range(NX)], axis=0)
        total = jnp.concatenate([st_x[e, cut, 1:2] for e in range(NX)], axis=0)
        top = jnp.max(jnp.where(is_held, peak, FLOOR), axis=0, keepdims=True)
        w = jnp.where(is_held, jnp.exp(peak - top), 0.0)
        coarse = w.astype(BF16)
        ws.append((coarse, (w - coarse.astype(F32)).astype(BF16)))
        zst_send[hh : hh + 1, :] = top
        zst_send[PAIR + hh : PAIR + hh + 1, :] = jnp.sum(w * total, axis=0, keepdims=True)
    for dz in FAR_FIRST:
        remote(zst_send, zst.at[NZ - dz], szs, rzs, at(dz, 0))
    zst[0] = zst_send[...]

    arrived(o_x.at[pl.ds(1, NX - 1)], ro)
    for hh in range(PAIR):
        data = jnp.concatenate(
            [o_x[e, hh * SLOTS : (hh + 1) * SLOTS, :] for e in range(NX)], axis=0
        )
        both = dot(ws[hh][0], data, ((0,), (0,))) + dot(ws[hh][1], data, ((0,), (0,)))
        part[:, hh * HD : (hh + 1) * HD] = both.astype(BF16)
    for dz in FAR_FIRST:
        remote(part.at[rows_of((mine + dz) % NT, BAND)], rs.at[NZ - dz], srs, rrs, at(dz, 0))
    my_band = rows_of(mine, BAND)
    rs[0] = part[my_band, :]

    arrived(wall.at[pl.ds(0, 3)], rw.at[0])
    for dt in (2, 6, 4):
        origin = (t + dt) % NT
        remote(wall.at[origin], wall.at[origin], sw.at[1], rw.at[1], sibling)

    arrived(qall.at[0, pl.ds(0, NZ - 1)], sq)
    arrived(qall.at[pl.ds(0, NX - 1)], sqx)
    arrived(wall.at[pl.ds(0, 3)], sw.at[0])
    arrived(st_x.at[pl.ds(0, NX - 1)], sst)
    arrived(o_x.at[pl.ds(0, NX - 1)], so)
    arrived(zst.at[pl.ds(0, NZ - 1)], szs)

    arrived(zst.at[pl.ds(1, NZ - 1)], rzs)
    scales = []
    for hh in range(PAIR):
        top = jnp.concatenate([zst[e, hh : hh + 1, :] for e in range(NZ)], axis=0)
        total = jnp.concatenate(
            [zst[e, PAIR + hh : PAIR + hh + 1, :] for e in range(NZ)], axis=0
        )
        highest = jnp.max(top, axis=0, keepdims=True)
        w = jnp.exp(top - highest)
        scales.append(w / jnp.sum(w * total, axis=0, keepdims=True))
    pad = jnp.zeros((ROWS - PAIR * NZ, ROWS), F32)
    scale_t[...] = jnp.transpose(jnp.concatenate(scales + [pad], axis=0))
    cols = scale_t[my_band, :]
    for e in range(NZ):
        for hh in range(PAIR):
            zw[e, :, hh * HD : (hh + 1) * HD] = jnp.broadcast_to(
                cols[:, hh * NZ + e : hh * NZ + e + 1], (BAND, HD)
            )
    arrived(rs.at[pl.ds(1, NZ - 1)], rrs)
    acc = jnp.zeros((BAND, PAIR * HD), F32)
    for e in range(NZ):
        acc = acc + rs[e].astype(F32) * zw[e]
    band[...] = acc.astype(BF16)

    @pl.when(mine != t)
    def _():
        pl.semaphore_wait(seen, 1)

    origin = t * NX + x
    along = 1 - 2 * (t % 2)

    def end(dz, dx):
        to = at(along * dz + NZ, dx)
        to["tp"] = mine
        return pltpu.make_async_remote_copy(
            src_ref=band,
            dst_ref=fin.at[origin],
            send_sem=sfin,
            recv_sem=rfin,
            device_id=to,
            device_id_type=MESH,
        )

    for dz, dx in ENDS:
        if (dz, dx) == (0, 0):

            @pl.when(mine != t)
            def _():
                end(0, 0).start()

            @pl.when(mine == t)
            def _():
                pltpu.make_async_copy(band, fin.at[origin], rfin).start()
        else:
            end(dz, dx).start()
    arrived(rs.at[pl.ds(0, NZ - 1)], srs)

    c_w.wait()
    arrived(wall.at[pl.ds(0, NX)], rw.at[1])
    arrived(wall.at[pl.ds(0, NX)], sw.at[1])
    arrived(fin, rfin)
    acc = jnp.zeros((BAND, HD), F32)
    for n in range(NT * NX):
        cut = slice((n % NX) * PAIR * HD, (n % NX + 1) * PAIR * HD)
        acc = acc + dot(fin[n], wall[n // NX, cut, :])
    out_ref[...] = acc.astype(BF16)
    arrived(fin.at[pl.ds(0, len(ENDS) - 1)], sfin)

    @pl.when(mine != t)
    def _():
        end(0, 0).wait_send()


def on_device(queries, key_cache, value_cache, out_weight, lengths, block_table):
    q = queries.reshape(2, GROUP, HD).transpose(1, 0, 2).reshape(2 * GROUP, HD)
    hbm = pl.BlockSpec(memory_space=pltpu.HBM)
    dma = pltpu.SemaphoreType.DMA
    vmem = pltpu.VMEM
    return pl.pallas_call(
        kernel,
        out_shape=jax.ShapeDtypeStruct((BAND, HD), BF16),
        in_specs=[hbm] * 6,
        out_specs=pl.BlockSpec(memory_space=pltpu.VMEM),
        scratch_shapes=[
            vmem((MAXB, ROWS), jnp.int32),
            vmem((1, ROWS), jnp.int32),
            vmem((SLOTS, BLK, HD), BF16),
            vmem((SLOTS, HD, BLK), BF16),
            vmem((SLOTS, BLK, HD), BF16),
            vmem((NX, NZ, 2 * GROUP, HD), BF16),
            vmem((ROWS, ROWS * GROUP), BF16),
            vmem((ROWS, ROWS), F32),
            vmem((NX * SLOTS, ROWS), F32),
            vmem((ROWS, BLK), F32),
            vmem((SLOTS, GROUP, BLK), BF16),
            vmem((ROWS, HD), F32),
            vmem((ROWS, HD), F32),
            vmem((ROWS, HD), BF16),
            vmem((NX, PAIR * SLOTS, HD), F32),
            vmem((NX, PAIR * SLOTS, HD), BF16),
            vmem((8, ROWS), F32),
            vmem((NZ, 8, ROWS), F32),
            vmem((ROWS, ROWS), F32),
            vmem((NZ, BAND, PAIR * HD), F32),
            vmem((ROWS, PAIR * HD), BF16),
            vmem((NZ, BAND, PAIR * HD), BF16),
            vmem((BAND, PAIR * HD), BF16),
            vmem((NT * NX, BAND, PAIR * HD), BF16),
            vmem((NT, GROUP * HD, HD), BF16),
            dma((6,)),
            dma,
            dma((len(LEGS),)),
            dma,
            dma,
            dma((2,)),
            dma((2,)),
            dma,
            dma,
            dma,
            dma,
            dma,
            dma,
            dma,
            dma,
            dma,
            dma,
            pltpu.SemaphoreType.REGULAR,
        ],
        compiler_params=pltpu.CompilerParams(
            collective_id=0, has_side_effects=True, vmem_limit_bytes=56 * 1024 * 1024
        ),
        cost_estimate=pl.CostEstimate(
            flops=400_000_000, bytes_accessed=5_000_000, transcendentals=70_000
        ),
        name="lent_attention",
    )(q, key_cache, value_cache, out_weight, lengths.reshape(1, ROWS), block_table.T)


def solution(mesh):
    return jax.shard_map(
        on_device,
        mesh=mesh,
        in_specs=(
            P("pool", "tp"),
            P("tp", "pool", None, None),
            P("tp", "pool", None, None),
            P("tp", "pool"),
            P(),
            P(),
        ),
        out_specs=P("tp", "pool"),
        check_vma=False,
    )
```

time: 57 us -> 53.2 us (0.933)
  Pallas kernels: 55.6 us -> 51.7 us
    pallas_call x1, Pallas kernels: 55.6 us -> 51.7 us  [on_device(): pl.pallas_call(kernel, out_shape=jax.ShapeDtypeStruct((BAND, HD), BF16),...]
where the time goes in v2:
time: 53.2 us; the launch traced here: 53 us
  Pallas kernels  51.7 us (97%)
  local copies, waits for them, and re-layouts  1.28 us (2%)
    pallas_call x1, Pallas kernels, on_device(): pl.pallas_call(kernel, out_shape=jax.ShapeDtypeStruct((BAND, HD), BF16),...  51.7 us
    unnamed x1, local copies, waits for them, and re-layouts  1.28 us

profile of v2, /device:TPU:1, one launch (start us, length us, event | category | flops | bytes accessed | tf_op | source)
XLA Modules:
  0.0 53.0 jit_solution(1443217663870745154)
XLA Ops:
  0.0 51.7 %lent_attention.1 = bf16[16,128]{1,0:T(8,128)(2,1)} custom-call(bf16[16,128]{1,0:T(8,128)(2,1)} %bitcast.8, bf16[1,16,512,128]{3,2,1,0:T(8,128)(2,1)} %k_hbm.1, bf16[1,16,512,128]{3,2,1,0:T(8,128)(2,1)} %v_hbm.1, bf16[1024,128]{1,0:T(8,128)(2,1)} %w_hbm.1, s32[1,128]{1,0:T(1,128)} %bitcast.9, s32[32,128]{1,0:T(8,128)} %bitcast.7), custom_call_target="tpu_custom_call" | custom-call | flops 400000000 | bytes 5000000 | tf_op jit(solution)/shard_map/lent_attention/pallas_call | solution.py:350
  51.7 1.3 %copy.9 = bf16[16,128]{1,0:T(8,128)(2,1)} copy(bf16[16,128]{1,0:T(8,128)(2,1)} %lent_attention.1) | data formatting | bytes 8192

commit v3 on v2

--- a/solution.py
+++ b/solution.py
@@ -52,6 +52,7 @@
     o_f,
     stat_f,
     o_send,
+    st_send,
     st_x,
     o_x,
     zst_send,
@@ -201,7 +202,7 @@
         score[cut] = dot(picked[cut].astype(BF16), keys_t[s])
     each = 4
     place_in = lax.broadcasted_iota(jnp.int32, (each * GROUP, BLK), 1).astype(F32)
-    first = lax.broadcasted_iota(jnp.int32, (GROUP, HD), 1) == 0
+    inverse = []
     for c in range(SLOTS // each):
         cut = slice(each * GROUP * c, each * GROUP * (c + 1))
         usable = place_in < lims[cut, 0:1]
@@ -209,19 +210,23 @@
         peak = jnp.max(scores, axis=1, keepdims=True)
         weights = jnp.where(usable, jnp.exp(scores - peak), 0.0)
         total = jnp.sum(weights, axis=1, keepdims=True)
+        used = total > 0.0
+        inverse.append(jnp.where(used, 1.0 / jnp.where(used, total, 1.0), 0.0))
+        level = jnp.where(used, peak + jnp.log(jnp.where(used, total, 1.0)), FLOOR)
         for i in range(each):
             s = each * c + i
             sl = slice(GROUP * i, GROUP * (i + 1))
             prob[s] = weights[sl].astype(BF16)
-            stat_f[pl.ds(s, GROUP, stride=SLOTS), :] = jnp.where(first, peak[sl], total[sl])
+            stat_f[pl.ds(s, GROUP, stride=SLOTS), :] = jnp.broadcast_to(level[sl], (GROUP, HD))
     mine_x = rows_of(x, PAIR * SLOTS)
+    st_send[...] = jnp.transpose(stat_f[...])[0:1, :]
     for dx in (2, 1, 3):
-        rows = rows_of((x + dx) % NX, PAIR * SLOTS)
-        remote(stat_f.at[rows], st_x.at[(NX - dx) % NX], sst, rst, at(0, dx))
-    st_x[0] = stat_f[mine_x, :]
+        remote(st_send, st_x.at[(NX - dx) % NX], sst, rst, at(0, dx))
+    st_x[0] = st_send[...]
     c_v.wait()
     for s in range(SLOTS):
-        o_f[pl.ds(s, GROUP, stride=SLOTS), :] = dot(prob[s], vals[s])
+        sl = slice(GROUP * (s % each), GROUP * (s % each + 1))
+        o_f[pl.ds(s, GROUP, stride=SLOTS), :] = dot(prob[s], vals[s]) * inverse[s // each][sl]
     o_send[...] = o_f[...].astype(BF16)
     for dx in (2, 1, 3):
         rows = rows_of((x + dx) % NX, PAIR * SLOTS)
@@ -229,18 +234,23 @@
     o_x[0] = o_send[mine_x, :]
 
     arrived(st_x.at[pl.ds(1, NX - 1)], rst)
+    pad = jnp.zeros((ROWS - NX, ROWS), F32)
+    stat_f[...] = jnp.transpose(jnp.concatenate([st_x[e] for e in range(NX)] + [pad], axis=0))
+    own = stat_f[mine_x, :]
     ws = []
     is_held = hold[...] > 0.0
     for hh in range(PAIR):
         cut = slice(hh * SLOTS, (hh + 1) * SLOTS)
-        peak = jnp.concatenate([st_x[e, cut, 0:1] for e in range(NX)], axis=0)
-        total = jnp.concatenate([st_x[e, cut, 1:2] for e in range(NX)], axis=0)
-        top = jnp.max(jnp.where(is_held, peak, FLOOR), axis=0, keepdims=True)
-        w = jnp.where(is_held, jnp.exp(peak - top), 0.0)
+        level = jnp.concatenate([own[cut, e : e + 1] for e in range(NX)], axis=0)
+        top = jnp.max(jnp.where(is_held, level, FLOOR), axis=0, keepdims=True)
+        w = jnp.where(is_held, jnp.exp(level - top), 0.0)
+        total = jnp.sum(w, axis=0, keepdims=True)
+        used = total > 0.0
+        total = jnp.where(used, total, 1.0)
+        w = w / total
         coarse = w.astype(BF16)
         ws.append((coarse, (w - coarse.astype(F32)).astype(BF16)))
-        zst_send[hh : hh + 1, :] = top
-        zst_send[PAIR + hh : PAIR + hh + 1, :] = jnp.sum(w * total, axis=0, keepdims=True)
+        zst_send[hh : hh + 1, :] = jnp.where(used, top + jnp.log(total), FLOOR)
     for dz in FAR_FIRST:
         remote(zst_send, zst.at[NZ - dz], szs, rzs, at(dz, 0))
     zst[0] = zst_send[...]
@@ -272,13 +282,9 @@
     arrived(zst.at[pl.ds(1, NZ - 1)], rzs)
     scales = []
     for hh in range(PAIR):
-        top = jnp.concatenate([zst[e, hh : hh + 1, :] for e in range(NZ)], axis=0)
-        total = jnp.concatenate(
-            [zst[e, PAIR + hh : PAIR + hh + 1, :] for e in range(NZ)], axis=0
-        )
-        highest = jnp.max(top, axis=0, keepdims=True)
-        w = jnp.exp(top - highest)
-        scales.append(w / jnp.sum(w * total, axis=0, keepdims=True))
+        level = jnp.concatenate([zst[e, hh : hh + 1, :] for e in range(NZ)], axis=0)
+        w = jnp.exp(level - jnp.max(level, axis=0, keepdims=True))
+        scales.append(w / jnp.sum(w, axis=0, keepdims=True))
     pad = jnp.zeros((ROWS - PAIR * NZ, ROWS), F32)
     scale_t[...] = jnp.transpose(jnp.concatenate(scales + [pad], axis=0))
     cols = scale_t[my_band, :]
@@ -297,7 +303,6 @@
     def _():
         pl.semaphore_wait(seen, 1)
 
-    origin = t * NX + x
     along = 1 - 2 * (t % 2)
 
     def end(dz, dx):
@@ -305,9 +310,9 @@
         to["tp"] = mine
         return pltpu.make_async_remote_copy(
             src_ref=band,
-            dst_ref=fin.at[origin],
+            dst_ref=fin.at[(NX - dx) % NX, t],
             send_sem=sfin,
-            recv_sem=rfin,
+            recv_sem=rfin.at[(NX - dx) % NX],
             device_id=to,
             device_id_type=MESH,
         )
@@ -321,7 +326,7 @@
 
             @pl.when(mine == t)
             def _():
-                pltpu.make_async_copy(band, fin.at[origin], rfin).start()
+                pltpu.make_async_copy(band, fin.at[0, t], rfin.at[0]).start()
         else:
             end(dz, dx).start()
     arrived(rs.at[pl.ds(0, NZ - 1)], srs)
@@ -329,13 +334,15 @@
     c_w.wait()
     arrived(wall.at[pl.ds(0, NX)], rw.at[1])
     arrived(wall.at[pl.ds(0, NX)], sw.at[1])
-    arrived(fin, rfin)
     acc = jnp.zeros((BAND, HD), F32)
-    for n in range(NT * NX):
-        cut = slice((n % NX) * PAIR * HD, (n % NX + 1) * PAIR * HD)
-        acc = acc + dot(fin[n], wall[n // NX, cut, :])
+    for e in (0, 1, 3, 2):
+        arrived(fin.at[e], rfin.at[e])
+        rows = rows_of((x + e) % NX, PAIR * HD)
+        for n in range(NT):
+            acc = acc + dot(fin[e, n], wall[n, rows, :])
     out_ref[...] = acc.astype(BF16)
-    arrived(fin.at[pl.ds(0, len(ENDS) - 1)], sfin)
+    arrived(fin.at[pl.ds(0, NX - 1)], sfin)
+    arrived(fin.at[0, pl.ds(0, NT - 1)], sfin)
 
     @pl.when(mine != t)
     def _():
@@ -349,7 +356,7 @@
     vmem = pltpu.VMEM
     return pl.pallas_call(
         kernel,
-        out_shape=jax.ShapeDtypeStruct((BAND, HD), BF16),
+        out_shape=pltpu.VMEM((BAND, HD), BF16),
         in_specs=[hbm] * 6,
         out_specs=pl.BlockSpec(memory_space=pltpu.VMEM),
         scratch_shapes=[
@@ -367,16 +374,17 @@
             vmem((ROWS, HD), F32),
             vmem((ROWS, HD), F32),
             vmem((ROWS, HD), BF16),
-            vmem((NX, PAIR * SLOTS, HD), F32),
+            vmem((1, ROWS), F32),
+            vmem((NX, 1, ROWS), F32),
             vmem((NX, PAIR * SLOTS, HD), BF16),
-            vmem((8, ROWS), F32),
-            vmem((NZ, 8, ROWS), F32),
+            vmem((PAIR, ROWS), F32),
+            vmem((NZ, PAIR, ROWS), F32),
             vmem((ROWS, ROWS), F32),
             vmem((NZ, BAND, PAIR * HD), F32),
             vmem((ROWS, PAIR * HD), BF16),
             vmem((NZ, BAND, PAIR * HD), BF16),
             vmem((BAND, PAIR * HD), BF16),
-            vmem((NT * NX, BAND, PAIR * HD), BF16),
+            vmem((NX, NT, BAND, PAIR * HD), BF16),
             vmem((NT, GROUP * HD, HD), BF16),
             dma((6,)),
             dma,
@@ -394,7 +402,7 @@
             dma,
             dma,
             dma,
-            dma,
+            dma((NX,)),
             pltpu.SemaphoreType.REGULAR,
         ],
         compiler_params=pltpu.CompilerParams(

time: 53.2 us -> 50.7 us (0.953)
  Pallas kernels: 51.7 us -> 50 us
  local copies, waits for them, and re-layouts: 1.28 us -> 0.6 us
    pallas_call x1, Pallas kernels: 51.7 us -> 50 us  [on_device(): pl.pallas_call(kernel, out_shape=pltpu.VMEM((BAND, HD), BF16), in_specs=[...]
    unnamed x1, local copies, waits for them, and re-layouts: 1.28 us -> 0.6 us
where the time goes in v3:
time: 50.7 us; the launch traced here: 50.6 us
  Pallas kernels  50 us (99%)
  local copies, waits for them, and re-layouts  0.6 us (1%)
    pallas_call x1, Pallas kernels, on_device(): pl.pallas_call(kernel, out_shape=pltpu.VMEM((BAND, HD), BF16), in_specs=[...  50 us

profile of v3, /device:TPU:1, one launch (start us, length us, event | category | flops | bytes accessed | tf_op | source)
XLA Modules:
  0.0 50.6 jit_solution(17712200507269150317)
XLA Ops:
  0.0 50.0 %lent_attention.1 = bf16[16,128]{1,0:T(8,128)(2,1)S(1)} custom-call(bf16[16,128]{1,0:T(8,128)(2,1)} %bitcast.8, bf16[1,16,512,128]{3,2,1,0:T(8,128)(2,1)} %k_hbm.1, bf16[1,16,512,128]{3,2,1,0:T(8,128)(2,1)} %v_hbm.1, bf16[1024,128]{1,0:T(8,128)(2,1)} %w_hbm.1, s32[1,128]{1,0:T(1,128)} %bitcast.9, s32[32,128]{1,0:T(8,128)} %bitcast.7), custom_call_target="tpu_custom_call" | custom-call | flops 400000000 | bytes 5000000 | tf_op jit(solution)/shard_map/lent_attention/pallas_call | solution.py:357
  50.0 0.6 %copy.9 = bf16[16,128]{1,0:T(8,128)(2,1)} copy(bf16[16,128]{1,0:T(8,128)(2,1)S(1)} %lent_attention.1) | data formatting | bytes 8192

commit v4 on v3

--- a/solution.py
+++ b/solution.py
@@ -17,14 +17,9 @@
 ROWS, SLOTS, BLK, HD, GROUP, MAXB = 128, 16, 512, 128, 8, 32
 PAIR = GROUP // NX
 BAND = ROWS // NT
-ZORDER = [0, 1, 2, 3, 4, 15, 14, 13, 12, 5, 6, 11, 10, 7, 8, 9]
-LEGS = ((0, 9), (9, 13), (13, 16))
+ZORDER = [0, 1, 2, 15, 14, 3, 4, 13, 12, 5, 6, 11, 10, 7, 8, 9]
+LEGS = ((0, 5), (5, 9), (9, 13), (13, 16))
 FAR_FIRST = (8, 7, 9, 6, 10, 5, 11, 4, 12, 3, 13, 2, 14, 1, 15)
-ENDS = sorted(
-    [(dz, dx) for dz in range(-3, 5) for dx in range(NX)],
-    key=lambda d: -(abs(d[0]) + min(d[1], NX - d[1])),
-)
-
 
 def dot(a, b, dims=((1,), (0,))):
     return lax.dot_general(a, b, (dims, ((), ())), preferred_element_type=F32)
@@ -139,11 +134,6 @@
     for dz in FAR_FIRST:
         k = place[NZ - dz]
         remote(qall.at[0, 0], qall.at[0, k], sq, rq.at[leg_of[k]], at(dz, 0))
-    sibling = {"pool": pool, "tp": t + 1 - 2 * (t % 2)}
-    for dt in (2, 6, 4):
-        remote(w_hbm, wall.at[t], sw.at[0], rw.at[0], {"pool": pool, "tp": (t + dt) % NT})
-    remote(w_hbm, wall.at[t], sw.at[1], rw.at[1], sibling)
-
     c_tab.wait()
     c_len.wait()
     tab_t = tab[...].astype(F32)
@@ -183,6 +173,11 @@
         for dx in (2, 1, 3):
             cut = pl.ds(lo, hi - lo)
             remote(qall.at[0, cut], qall.at[(NX - dx) % NX, cut], sqx, rqx, at(0, dx))
+    sibling = {"pool": pool, "tp": t + 1 - 2 * (t % 2)}
+    for dt in (2, 6, 4):
+        remote(w_hbm, wall.at[t], sw.at[0], rw.at[0], {"pool": pool, "tp": (t + dt) % NT})
+    remote(w_hbm, wall.at[t], sw.at[1], rw.at[1], sibling)
+
     c_k.wait()
     for s in range(SLOTS):
         keys_t[s] = keys[s].T
@@ -303,32 +298,37 @@
     def _():
         pl.semaphore_wait(seen, 1)
 
-    along = 1 - 2 * (t % 2)
-
-    def end(dz, dx):
-        to = at(along * dz + NZ, dx)
-        to["tp"] = mine
-        return pltpu.make_async_remote_copy(
+    reach = NZ // 2
+    lowest = (z - 3 - t % 2 + NZ) % NZ
+    skip = (NZ - lowest) * (lowest // (reach + 1))
+
+    def end(step, dx):
+        zz = (lowest + (step + skip) % reach) % NZ
+        return zz, pltpu.make_async_remote_copy(
             src_ref=band,
             dst_ref=fin.at[(NX - dx) % NX, t],
             send_sem=sfin,
             recv_sem=rfin.at[(NX - dx) % NX],
-            device_id=to,
+            device_id={"pool": zz * NX + (x + dx) % NX, "tp": mine},
             device_id_type=MESH,
         )
 
-    for dz, dx in ENDS:
-        if (dz, dx) == (0, 0):
-
-            @pl.when(mine != t)
-            def _():
-                end(0, 0).start()
-
-            @pl.when(mine == t)
+    for step in range(reach):
+        for dx in (2, 1, 3, 0):
+            zz, copy = end(step, dx)
+            if dx:
+                copy.start()
+                continue
+            here = jnp.logical_and(zz == z, mine == t)
+
+            @pl.when(jnp.logical_not(here))
+            def _(copy=copy):
+                copy.start()
+
+            @pl.when(here)
             def _():
                 pltpu.make_async_copy(band, fin.at[0, t], rfin.at[0]).start()
-        else:
-            end(dz, dx).start()
+
     arrived(rs.at[pl.ds(0, NZ - 1)], srs)
 
     c_w.wait()
@@ -346,7 +346,7 @@
 
     @pl.when(mine != t)
     def _():
-        end(0, 0).wait_send()
+        end(0, 0)[1].wait_send()
 
 
 def on_device(queries, key_cache, value_cache, out_weight, lengths, block_table):

time: 50.7 us -> 48.4 us (0.955)
  Pallas kernels: 50 us -> 47.6 us
    pallas_call x1, Pallas kernels: 50 us -> 47.6 us  [on_device(): pl.pallas_call(kernel, out_shape=pltpu.VMEM((BAND, HD), BF16), in_specs=[...]
where the time goes in v4:
time: 48.4 us; the launch traced here: 48.2 us
  Pallas kernels  47.6 us (98%)
  local copies, waits for them, and re-layouts  0.6 us (1%)
    pallas_call x1, Pallas kernels, on_device(): pl.pallas_call(kernel, out_shape=pltpu.VMEM((BAND, HD), BF16), in_specs=[...  47.6 us

profile of v4, /device:TPU:1, one launch (start us, length us, event | category | flops | bytes accessed | tf_op | source)
XLA Modules:
  0.0 48.2 jit_solution(15968862071395431606)
XLA Ops:
  0.0 47.6 %lent_attention.1 = bf16[16,128]{1,0:T(8,128)(2,1)S(1)} custom-call(bf16[16,128]{1,0:T(8,128)(2,1)} %bitcast.8, bf16[1,16,512,128]{3,2,1,0:T(8,128)(2,1)} %k_hbm.1, bf16[1,16,512,128]{3,2,1,0:T(8,128)(2,1)} %v_hbm.1, bf16[1024,128]{1,0:T(8,128)(2,1)} %w_hbm.1, s32[1,128]{1,0:T(1,128)} %bitcast.9, s32[32,128]{1,0:T(8,128)} %bitcast.7), custom_call_target="tpu_custom_call" | custom-call | flops 400000000 | bytes 5000000 | tf_op jit(solution)/shard_map/lent_attention/pallas_call | solution.py:357
  47.6 0.6 %copy.9 = bf16[16,128]{1,0:T(8,128)(2,1)} copy(bf16[16,128]{1,0:T(8,128)(2,1)S(1)} %lent_attention.1) | data formatting | bytes 8192

commit v5 on v4

--- a/solution.py
+++ b/solution.py
@@ -17,8 +17,11 @@
 ROWS, SLOTS, BLK, HD, GROUP, MAXB = 128, 16, 512, 128, 8, 32
 PAIR = GROUP // NX
 BAND = ROWS // NT
-ZORDER = [0, 1, 2, 15, 14, 3, 4, 13, 12, 5, 6, 11, 10, 7, 8, 9]
-LEGS = ((0, 5), (5, 9), (9, 13), (13, 16))
+HUB = 4
+ZORDER = [0, 1, 2, 3, 4, 15, 14, 13, 12, 5, 6, 7, 11, 10, 9, 8]
+UP, DOWN, FAR_UP, FAR_DOWN = (1, 5), (5, 9), (9, 12), (12, 16)
+NEAR = (4, 12, 3, 13, 2, 14, 1, 15)
+SPREAD = 5
 FAR_FIRST = (8, 7, 9, 6, 10, 5, 11, 4, 12, 3, 13, 2, 14, 1, 15)
 
 def dot(a, b, dims=((1,), (0,))):
@@ -82,10 +85,13 @@
     t = lax.axis_index("tp")
     z = pool // NX
     x = pool % NX
-    mine = (z + 3 * t) % NT
+    theirs = (z + (NT - SPREAD) * t) % NT
 
     def at(dz, dx):
         return {"pool": ((z + dz) % NZ) * NX + (x + dx) % NX, "tp": t}
+
+    def finisher(dz):
+        return SPREAD * (z + dz + NT - t) % NT
 
     def remote(src, dst, send, recv, to):
         copy = pltpu.make_async_remote_copy(
@@ -106,7 +112,7 @@
         pltpu.make_async_copy(ref, ref, sem).wait()
 
     barrier = pltpu.get_barrier_semaphore()
-    for dz in FAR_FIRST:
+    for dz in NEAR:
         pl.semaphore_signal(barrier, inc=1, device_id=at(dz, 0), device_id_type=MESH)
     c_q = pltpu.make_async_copy(q_hbm, qall.at[0, 0], loc_sem.at[2])
     c_q.start()
@@ -127,13 +133,13 @@
     c_v.start()
     c_w.start()
     c_q.wait()
-    pl.semaphore_wait(barrier, NZ - 1 + NX - 1 + NT - 1)
+    pl.semaphore_wait(barrier, len(NEAR) + NX - 1 + NT - 1)
 
     place = {dz: k for k, dz in enumerate(ZORDER)}
-    leg_of = [n for n, (lo, hi) in enumerate(LEGS) for k in range(lo, hi)]
-    for dz in FAR_FIRST:
+    for dz in NEAR:
         k = place[NZ - dz]
-        remote(qall.at[0, 0], qall.at[0, k], sq, rq.at[leg_of[k]], at(dz, 0))
+        remote(qall.at[0, 0], qall.at[0, k], sq, rq.at[int(k >= DOWN[0])], at(dz, 0))
+
     c_tab.wait()
     c_len.wait()
     tab_t = tab[...].astype(F32)
@@ -167,12 +173,25 @@
         cut = slice(c * 128, (c + 1) * 128)
         sel[:, cut] = jnp.where(key_col == key_row[:, cut], 1.0, 0.0).astype(BF16)
 
-    for lo, hi in LEGS:
-        new = max(lo, 1)
-        arrived(qall.at[0, pl.ds(new, hi - new)], rq.at[LEGS.index((lo, hi))])
+    def pieces(cut):
+        return pl.ds(cut[0], cut[1] - cut[0])
+
+    def across(cut):
         for dx in (2, 1, 3):
-            cut = pl.ds(lo, hi - lo)
-            remote(qall.at[0, cut], qall.at[(NX - dx) % NX, cut], sqx, rqx, at(0, dx))
+            remote(
+                qall.at[0, pieces(cut)], qall.at[(NX - dx) % NX, pieces(cut)], sqx, rqx, at(0, dx)
+            )
+
+    arrived(qall.at[0, pieces(DOWN)], rq.at[1])
+    remote(qall.at[0, pieces(DOWN)], qall.at[0, pieces(FAR_DOWN)], sq, rq.at[3], at(HUB, 0))
+    arrived(qall.at[0, pieces(UP)], rq.at[0])
+    count = pl.ds(UP[0], FAR_UP[1] - FAR_UP[0])
+    remote(qall.at[0, count], qall.at[0, pieces(FAR_UP)], sq, rq.at[2], at(NZ - HUB, 0))
+    across((0, DOWN[1]))
+    arrived(qall.at[0, pieces(FAR_UP)], rq.at[2])
+    across(FAR_UP)
+    arrived(qall.at[0, pieces(FAR_DOWN)], rq.at[3])
+    across(FAR_DOWN)
     sibling = {"pool": pool, "tp": t + 1 - 2 * (t % 2)}
     for dt in (2, 6, 4):
         remote(w_hbm, wall.at[t], sw.at[0], rw.at[0], {"pool": pool, "tp": (t + dt) % NT})
@@ -182,12 +201,9 @@
     for s in range(SLOTS):
         keys_t[s] = keys[s].T
     arrived(qall.at[pl.ds(1, NX - 1)], rqx)
-    teller = 3 * (t - z + NZ) % NT
-
-    @pl.when(teller != t)
-    def _():
+    for dt in (4, 3, 5, 2, 6, 1, 7):
         pl.semaphore_signal(
-            seen, inc=1, device_id={"pool": pool, "tp": teller}, device_id_type=MESH
+            seen, inc=1, device_id={"pool": pool, "tp": (t + dt) % NT}, device_id_type=MESH
         )
 
     picked = dot(sel[...], qall[...].reshape(ROWS * GROUP, HD))
@@ -246,9 +262,30 @@
         coarse = w.astype(BF16)
         ws.append((coarse, (w - coarse.astype(F32)).astype(BF16)))
         zst_send[hh : hh + 1, :] = jnp.where(used, top + jnp.log(total), FLOOR)
-    for dz in FAR_FIRST:
-        remote(zst_send, zst.at[NZ - dz], szs, rzs, at(dz, 0))
-    zst[0] = zst_send[...]
+    pl.semaphore_wait(seen, NT - 1)
+
+    def hand(dz, source, target, send, recv):
+        to = at(dz, 0)
+        to["tp"] = finisher(dz)
+        if dz:
+            remote(source, target, send, recv, to)
+            return
+
+        @pl.when(finisher(0) != t)
+        def _():
+            remote(source, target, send, recv, to)
+
+        @pl.when(finisher(0) == t)
+        def _():
+            pltpu.make_async_copy(source, target, recv).start()
+
+    def left_here(ref, send):
+        @pl.when(finisher(0) != t)
+        def _():
+            arrived(ref, send)
+
+    for dz in FAR_FIRST + (0,):
+        hand(dz, zst_send, zst.at[(NZ - dz) % NZ], szs, rzs)
 
     arrived(o_x.at[pl.ds(1, NX - 1)], ro)
     for hh in range(PAIR):
@@ -257,10 +294,9 @@
         )
         both = dot(ws[hh][0], data, ((0,), (0,))) + dot(ws[hh][1], data, ((0,), (0,)))
         part[:, hh * HD : (hh + 1) * HD] = both.astype(BF16)
-    for dz in FAR_FIRST:
-        remote(part.at[rows_of((mine + dz) % NT, BAND)], rs.at[NZ - dz], srs, rrs, at(dz, 0))
-    my_band = rows_of(mine, BAND)
-    rs[0] = part[my_band, :]
+    for dz in FAR_FIRST + (0,):
+        hand(dz, part.at[rows_of(finisher(dz), BAND)], rs.at[(NZ - dz) % NZ], srs, rrs)
+    my_band = rows_of(t, BAND)
 
     arrived(wall.at[pl.ds(0, 3)], rw.at[0])
     for dt in (2, 6, 4):
@@ -273,8 +309,9 @@
     arrived(st_x.at[pl.ds(0, NX - 1)], sst)
     arrived(o_x.at[pl.ds(0, NX - 1)], so)
     arrived(zst.at[pl.ds(0, NZ - 1)], szs)
-
-    arrived(zst.at[pl.ds(1, NZ - 1)], rzs)
+    left_here(zst.at[0], szs)
+
+    arrived(zst, rzs)
     scales = []
     for hh in range(PAIR):
         level = jnp.concatenate([zst[e, hh : hh + 1, :] for e in range(NZ)], axis=0)
@@ -288,16 +325,12 @@
             zw[e, :, hh * HD : (hh + 1) * HD] = jnp.broadcast_to(
                 cols[:, hh * NZ + e : hh * NZ + e + 1], (BAND, HD)
             )
-    arrived(rs.at[pl.ds(1, NZ - 1)], rrs)
+    arrived(rs, rrs)
     acc = jnp.zeros((BAND, PAIR * HD), F32)
     for e in range(NZ):
         acc = acc + rs[e].astype(F32) * zw[e]
     band[...] = acc.astype(BF16)
 
-    @pl.when(mine != t)
-    def _():
-        pl.semaphore_wait(seen, 1)
-
     reach = NZ // 2
     lowest = (z - 3 - t % 2 + NZ) % NZ
     skip = (NZ - lowest) * (lowest // (reach + 1))
@@ -306,10 +339,10 @@
         zz = (lowest + (step + skip) % reach) % NZ
         return zz, pltpu.make_async_remote_copy(
             src_ref=band,
-            dst_ref=fin.at[(NX - dx) % NX, t],
+            dst_ref=fin.at[(NX - dx) % NX, theirs],
             send_sem=sfin,
             recv_sem=rfin.at[(NX - dx) % NX],
-            device_id={"pool": zz * NX + (x + dx) % NX, "tp": mine},
+            device_id={"pool": zz * NX + (x + dx) % NX, "tp": t},
             device_id_type=MESH,
         )
 
@@ -319,17 +352,14 @@
             if dx:
                 copy.start()
                 continue
-            here = jnp.logical_and(zz == z, mine == t)
-
-            @pl.when(jnp.logical_not(here))
+
+            @pl.when(zz != z)
             def _(copy=copy):
                 copy.start()
 
-            @pl.when(here)
-            def _():
-                pltpu.make_async_copy(band, fin.at[0, t], rfin.at[0]).start()
-
+    pltpu.make_async_copy(band, fin.at[0, theirs], rfin.at[0]).start()
     arrived(rs.at[pl.ds(0, NZ - 1)], srs)
+    left_here(rs.at[0], srs)
 
     c_w.wait()
     arrived(wall.at[pl.ds(0, NX)], rw.at[1])
@@ -343,10 +373,6 @@
     out_ref[...] = acc.astype(BF16)
     arrived(fin.at[pl.ds(0, NX - 1)], sfin)
     arrived(fin.at[0, pl.ds(0, NT - 1)], sfin)
-
-    @pl.when(mine != t)
-    def _():
-        end(0, 0)[1].wait_send()
 
 
 def on_device(queries, key_cache, value_cache, out_weight, lengths, block_table):
@@ -388,7 +414,7 @@
             vmem((NT, GROUP * HD, HD), BF16),
             dma((6,)),
             dma,
-            dma((len(LEGS),)),
+            dma((4,)),
             dma,
             dma,
             dma((2,)),

time: 48.4 us -> 47.7 us (0.986); the launches traced: 48.2 us -> 46.9 us
  Pallas kernels: 47.6 us -> 46.3 us
    pallas_call x1, Pallas kernels: 47.6 us -> 46.3 us  [on_device(): pl.pallas_call(kernel, out_shape=pltpu.VMEM((BAND, HD), BF16), in_specs=[...]
where the time goes in v5:
time: 47.7 us; the launch traced here: 46.9 us
  Pallas kernels  46.3 us (97%)
  local copies, waits for them, and re-layouts  0.6 us (1%)
    pallas_call x1, Pallas kernels, on_device(): pl.pallas_call(kernel, out_shape=pltpu.VMEM((BAND, HD), BF16), in_specs=[...  46.3 us

profile of v5, /device:TPU:1, one launch (start us, length us, event | category | flops | bytes accessed | tf_op | source)
XLA Modules:
  0.0 46.9 jit_solution(8343464086977906106)
XLA Ops:
  0.0 46.3 %lent_attention.1 = bf16[16,128]{1,0:T(8,128)(2,1)S(1)} custom-call(bf16[16,128]{1,0:T(8,128)(2,1)} %bitcast.8, bf16[1,16,512,128]{3,2,1,0:T(8,128)(2,1)} %k_hbm.1, bf16[1,16,512,128]{3,2,1,0:T(8,128)(2,1)} %v_hbm.1, bf16[1024,128]{1,0:T(8,128)(2,1)} %w_hbm.1, s32[1,128]{1,0:T(1,128)} %bitcast.9, s32[32,128]{1,0:T(8,128)} %bitcast.7), custom_call_target="tpu_custom_call" | custom-call | flops 400000000 | bytes 5000000 | tf_op jit(solution)/shard_map/lent_attention/pallas_call | solution.py:383
  46.3 0.6 %copy.9 = bf16[16,128]{1,0:T(8,128)(2,1)} copy(bf16[16,128]{1,0:T(8,128)(2,1)S(1)} %lent_attention.1) | data formatting | bytes 8192

commit v6 on v5

--- a/solution.py
+++ b/solution.py
@@ -140,6 +140,11 @@
         k = place[NZ - dz]
         remote(qall.at[0, 0], qall.at[0, k], sq, rq.at[int(k >= DOWN[0])], at(dz, 0))
 
+    sibling = {"pool": pool, "tp": t + 1 - 2 * (t % 2)}
+    for dt in (2, 6, 4):
+        remote(w_hbm, wall.at[t], sw.at[0], rw.at[0], {"pool": pool, "tp": (t + dt) % NT})
+    remote(w_hbm, wall.at[t], sw.at[1], rw.at[1], sibling)
+
     c_tab.wait()
     c_len.wait()
     tab_t = tab[...].astype(F32)
@@ -192,11 +197,6 @@
     across(FAR_UP)
     arrived(qall.at[0, pieces(FAR_DOWN)], rq.at[3])
     across(FAR_DOWN)
-    sibling = {"pool": pool, "tp": t + 1 - 2 * (t % 2)}
-    for dt in (2, 6, 4):
-        remote(w_hbm, wall.at[t], sw.at[0], rw.at[0], {"pool": pool, "tp": (t + dt) % NT})
-    remote(w_hbm, wall.at[t], sw.at[1], rw.at[1], sibling)
-
     c_k.wait()
     for s in range(SLOTS):
         keys_t[s] = keys[s].T

time: 47.7 us -> 47.4 us (level)
  the two profiles are of different devices: /device:TPU:1 before, /device:TPU:2 now
where the time goes in v6:
time: 47.4 us; the launch traced here: 47.3 us
  Pallas kernels  46.7 us (99%)
  local copies, waits for them, and re-layouts  0.6 us (1%)
    pallas_call x1, Pallas kernels, on_device(): pl.pallas_call(kernel, out_shape=pltpu.VMEM((BAND, HD), BF16), in_specs=[...  46.7 us

profile of v6, /device:TPU:2, one launch (start us, length us, event | category | flops | bytes accessed | tf_op | source)
XLA Modules:
  0.0 47.3 jit_solution(6275556470931940475)
XLA Ops:
  0.0 46.7 %lent_attention.1 = bf16[16,128]{1,0:T(8,128)(2,1)S(1)} custom-call(bf16[16,128]{1,0:T(8,128)(2,1)} %bitcast.8, bf16[1,16,512,128]{3,2,1,0:T(8,128)(2,1)} %k_hbm.1, bf16[1,16,512,128]{3,2,1,0:T(8,128)(2,1)} %v_hbm.1, bf16[1024,128]{1,0:T(8,128)(2,1)} %w_hbm.1, s32[1,128]{1,0:T(1,128)} %bitcast.9, s32[32,128]{1,0:T(8,128)} %bitcast.7), custom_call_target="tpu_custom_call" | custom-call | flops 400000000 | bytes 5000000 | tf_op jit(solution)/shard_map/lent_attention/pallas_call | solution.py:383
  46.7 0.6 %copy.9 = bf16[16,128]{1,0:T(8,128)(2,1)} copy(bf16[16,128]{1,0:T(8,128)(2,1)S(1)} %lent_attention.1) | data formatting | bytes 8192

commit v7 on v6

--- a/solution.py
+++ b/solution.py
@@ -48,7 +48,6 @@
     score,
     prob,
     o_f,
-    stat_f,
     o_send,
     st_send,
     st_x,
@@ -214,6 +213,8 @@
     each = 4
     place_in = lax.broadcasted_iota(jnp.int32, (each * GROUP, BLK), 1).astype(F32)
     inverse = []
+    spot = sub % GROUP * SLOTS + sub // GROUP
+    levels = jnp.zeros((1, ROWS), F32)
     for c in range(SLOTS // each):
         cut = slice(each * GROUP * c, each * GROUP * (c + 1))
         usable = place_in < lims[cut, 0:1]
@@ -224,13 +225,15 @@
         used = total > 0.0
         inverse.append(jnp.where(used, 1.0 / jnp.where(used, total, 1.0), 0.0))
         level = jnp.where(used, peak + jnp.log(jnp.where(used, total, 1.0)), FLOOR)
+        levels = levels + jnp.sum(
+            jnp.where(lane[cut] == spot[cut], level, 0.0), axis=0, keepdims=True
+        )
         for i in range(each):
             s = each * c + i
             sl = slice(GROUP * i, GROUP * (i + 1))
             prob[s] = weights[sl].astype(BF16)
-            stat_f[pl.ds(s, GROUP, stride=SLOTS), :] = jnp.broadcast_to(level[sl], (GROUP, HD))
     mine_x = rows_of(x, PAIR * SLOTS)
-    st_send[...] = jnp.transpose(stat_f[...])[0:1, :]
+    st_send[...] = levels
     for dx in (2, 1, 3):
         remote(st_send, st_x.at[(NX - dx) % NX], sst, rst, at(0, dx))
     st_x[0] = st_send[...]
@@ -245,14 +248,15 @@
     o_x[0] = o_send[mine_x, :]
 
     arrived(st_x.at[pl.ds(1, NX - 1)], rst)
-    pad = jnp.zeros((ROWS - NX, ROWS), F32)
-    stat_f[...] = jnp.transpose(jnp.concatenate([st_x[e] for e in range(NX)] + [pad], axis=0))
-    own = stat_f[mine_x, :]
+    every = jnp.concatenate(
+        [jnp.broadcast_to(st_x[e], (SLOTS, ROWS)) for e in range(NX)], axis=0
+    )
+    lane4 = lax.broadcasted_iota(jnp.int32, (NX * SLOTS, ROWS), 1)
     ws = []
     is_held = hold[...] > 0.0
     for hh in range(PAIR):
-        cut = slice(hh * SLOTS, (hh + 1) * SLOTS)
-        level = jnp.concatenate([own[cut, e : e + 1] for e in range(NX)], axis=0)
+        mine = lane4 == (x * PAIR + hh) * SLOTS + sub4 % SLOTS
+        level = jnp.sum(jnp.where(mine, every, 0.0), axis=1, keepdims=True)
         top = jnp.max(jnp.where(is_held, level, FLOOR), axis=0, keepdims=True)
         w = jnp.where(is_held, jnp.exp(level - top), 0.0)
         total = jnp.sum(w, axis=0, keepdims=True)
@@ -332,7 +336,7 @@
     band[...] = acc.astype(BF16)
 
     reach = NZ // 2
-    lowest = (z - 3 - t % 2 + NZ) % NZ
+    lowest = (z - 4 + t % 2 + NZ) % NZ
     skip = (NZ - lowest) * (lowest // (reach + 1))
 
     def end(step, dx):
@@ -398,7 +402,6 @@
             vmem((ROWS, BLK), F32),
             vmem((SLOTS, GROUP, BLK), BF16),
             vmem((ROWS, HD), F32),
-            vmem((ROWS, HD), F32),
             vmem((ROWS, HD), BF16),
             vmem((1, ROWS), F32),
             vmem((NX, 1, ROWS), F32),

time: 47.4 us -> 47.1 us (level)
  the two profiles are of different devices: /device:TPU:2 before, /device:TPU:1 now
where the time goes in v7:
time: 47.1 us; the launch traced here: 46.2 us
  Pallas kernels  45.6 us (97%)
  local copies, waits for them, and re-layouts  0.6 us (1%)
    pallas_call x1, Pallas kernels, on_device(): pl.pallas_call(kernel, out_shape=pltpu.VMEM((BAND, HD), BF16), in_specs=[...  45.6 us

profile of v7, /device:TPU:1, one launch (start us, length us, event | category | flops | bytes accessed | tf_op | source)
XLA Modules:
  0.0 46.2 jit_solution(17523941926183463536)
XLA Ops:
  0.0 45.6 %lent_attention.1 = bf16[16,128]{1,0:T(8,128)(2,1)S(1)} custom-call(bf16[16,128]{1,0:T(8,128)(2,1)} %bitcast.8, bf16[1,16,512,128]{3,2,1,0:T(8,128)(2,1)} %k_hbm.1, bf16[1,16,512,128]{3,2,1,0:T(8,128)(2,1)} %v_hbm.1, bf16[1024,128]{1,0:T(8,128)(2,1)} %w_hbm.1, s32[1,128]{1,0:T(1,128)} %bitcast.9, s32[32,128]{1,0:T(8,128)} %bitcast.7), custom_call_target="tpu_custom_call" | custom-call | flops 400000000 | bytes 5000000 | tf_op jit(solution)/shard_map/lent_attention/pallas_call | solution.py:387
  45.6 0.6 %copy.9 = bf16[16,128]{1,0:T(8,128)(2,1)} copy(bf16[16,128]{1,0:T(8,128)(2,1)S(1)} %lent_attention.1) | data formatting | bytes 8192

commit v8 on v7

--- a/solution.py
+++ b/solution.py
@@ -183,7 +183,11 @@
     def across(cut):
         for dx in (2, 1, 3):
             remote(
-                qall.at[0, pieces(cut)], qall.at[(NX - dx) % NX, pieces(cut)], sqx, rqx, at(0, dx)
+                qall.at[0, pieces(cut)],
+                qall.at[(NX - dx) % NX, pieces(cut)],
+                sqx,
+                rqx.at[(NX - dx) % NX],
+                at(0, dx),
             )
 
     arrived(qall.at[0, pieces(DOWN)], rq.at[1])
@@ -199,13 +203,17 @@
     c_k.wait()
     for s in range(SLOTS):
         keys_t[s] = keys[s].T
-    arrived(qall.at[pl.ds(1, NX - 1)], rqx)
+    picked = jnp.zeros((ROWS, HD), F32)
+    for e in (0, 3, 1, 2):
+        if e:
+            arrived(qall.at[e], rqx.at[e])
+        cut = slice(e * NZ * 2 * GROUP, (e + 1) * NZ * 2 * GROUP)
+        picked = picked + dot(sel[:, cut], qall[e].reshape(NZ * 2 * GROUP, HD))
     for dt in (4, 3, 5, 2, 6, 1, 7):
         pl.semaphore_signal(
             seen, inc=1, device_id={"pool": pool, "tp": (t + dt) % NT}, device_id_type=MESH
         )
 
-    picked = dot(sel[...], qall[...].reshape(ROWS * GROUP, HD))
     scaling = 1.0 / math.sqrt(HD)
     for s in range(SLOTS):
         cut = slice(GROUP * s, GROUP * (s + 1))
@@ -419,7 +427,7 @@
             dma,
             dma((4,)),
             dma,
-            dma,
+            dma((NX,)),
             dma((2,)),
             dma((2,)),
             dma,

time: 47.1 us -> 47.1 us (level)
  no operation moved by 1% of the time
where the time goes in v8:
time: 47.1 us; the launch traced here: 46.5 us
  Pallas kernels  45.9 us (97%)
  local copies, waits for them, and re-layouts  0.6 us (1%)
    pallas_call x1, Pallas kernels, on_device(): pl.pallas_call(kernel, out_shape=pltpu.VMEM((BAND, HD), BF16), in_specs=[...  45.9 us

profile of v8, /device:TPU:1, one launch (start us, length us, event | category | flops | bytes accessed | tf_op | source)
XLA Modules:
  0.0 46.5 jit_solution(5608564261221904942)
XLA Ops:
  0.0 45.9 %lent_attention.1 = bf16[16,128]{1,0:T(8,128)(2,1)S(1)} custom-call(bf16[16,128]{1,0:T(8,128)(2,1)} %bitcast.8, bf16[1,16,512,128]{3,2,1,0:T(8,128)(2,1)} %k_hbm.1, bf16[1,16,512,128]{3,2,1,0:T(8,128)(2,1)} %v_hbm.1, bf16[1024,128]{1,0:T(8,128)(2,1)} %w_hbm.1, s32[1,128]{1,0:T(1,128)} %bitcast.9, s32[32,128]{1,0:T(8,128)} %bitcast.7), custom_call_target="tpu_custom_call" | custom-call | flops 400000000 | bytes 5000000 | tf_op jit(solution)/shard_map/lent_attention/pallas_call | solution.py:395
  45.9 0.6 %copy.9 = bf16[16,128]{1,0:T(8,128)(2,1)} copy(bf16[16,128]{1,0:T(8,128)(2,1)S(1)} %lent_attention.1) | data formatting | bytes 8192
